TPU v7x, 512 devices: a whole 4x8x8 slice. The times are simulated.
512 devices in a mesh: ctx: 64 (over x, y_lo, z), tp: 8 (over y_hi, core).
Axes of the slice: x: 4, y: 8 (y_hi: 4, y_lo: 2; y = y_hi * 2 + y_lo), z: 8, core: 2. Of those that a mesh axis runs over, the one named last changes fastest.
Arguments:
- queries: bfloat16 [8192, 5120], P('ctx', 'tp'), may hold values from -8 to 8
- keys: bfloat16 [16384, 1024], P('ctx', 'tp'), may hold values from -8 to 8
- values: bfloat16 [16384, 1024], P('ctx', 'tp'), may hold values from -6 to 6
- subtree_ends: int32 [16384], P('ctx'), may hold values from 1 to 16384, as said below
- query_positions: int32 [8192], P('ctx'), may hold values from 0 to 16383, as said below
- balance_route: int32 [64, 128], P('ctx'), may hold values from 0 to 127, each once within a row
- out_weight: bfloat16 [5120, 2560], P('tp'), may hold values from -0.3125 to 0.3125
Outputs:
- mixed: bfloat16 [8192, 2560], P(('ctx', 'tp'))
Inputs may be any that keep to these rules, and one draw needn't show every extreme that they name: Tokens are packed depth first: for every token k, each token j with k < j < subtree_ends[k] lies in the subtree of k, and subtree_ends[k] > k; token 0 is the root and subtree_ends[0] = 16384. `query_positions`: strictly increasing; query row i stands for a token among positions i * (2) to (i + 1) * 2 - 1. Each row is a permutation of 0 to 127: query row r of the device at ctx index s goes to owner balance_route[s, r] // 2, slot balance_route[s, r] % 2.
All inputs are finite; a program needn't handle non-finite values.
Results may differ from a plain program's by a relative error of at most 0.019.
Values may be sent and summed in bfloat16 or wider, within the bound.
A program may use at most 64 MiB of HBM per device.

v0:
```python
import math

import jax
import jax.numpy as jnp
from jax import lax
from jax.sharding import PartitionSpec as P

HEAD_SIZE = 128


def owner_order(rows, route_row):
    number = rows.shape[0]
    inverse = jnp.zeros((number,), jnp.int32).at[route_row].set(jnp.arange(number, dtype=jnp.int32))
    return jnp.take(rows, inverse, axis=0)


def attend(query_rows, query_pos, keys, values, subtree_ends):
    number = query_rows.shape[0]
    groups = keys.shape[1] // HEAD_SIZE
    ratio = query_rows.shape[1] // HEAD_SIZE // groups
    grouped = query_rows.reshape(number, groups, ratio, HEAD_SIZE)
    scale = 1.0 / math.sqrt(HEAD_SIZE)

    def compute(rows, visible, key_block, value_block, state):
        best, total, summed = state
        width = key_block.shape[0]
        scores = (
            jnp.einsum(
                "qgrd,kgd->qgrk",
                rows,
                key_block.reshape(width, groups, HEAD_SIZE),
                preferred_element_type=jnp.float32,
            )
            * scale
        )
        scores = jnp.where(visible[:, None, None, :], scores, -jnp.inf)
        newbest = jnp.maximum(best, jnp.max(scores, axis=-1))
        shifted = jnp.where(newbest == -jnp.inf, 0.0, newbest)
        weights = jnp.exp(scores - shifted[..., None])
        factor = jnp.exp(best - shifted)
        total = total * factor + jnp.sum(weights, axis=-1)
        update = jnp.einsum(
            "qgrk,kgd->qgrd",
            weights.astype(jnp.bfloat16),
            value_block.reshape(width, groups, HEAD_SIZE),
            preferred_element_type=jnp.float32,
        )
        summed = summed * factor[..., None] + update
        return (newbest, total, summed)

    def block_update(carry, key_block, value_block, end_block, first):
        width = key_block.shape[0]
        key_index = first + jnp.arange(width, dtype=jnp.int32)
        visible = (key_index[None, :] <= query_pos[:, None]) & (
            query_pos[:, None] < end_block[None, :]
        )
        return compute(grouped, visible, key_block, value_block, carry)

    initial = (
        jnp.full((number, groups, ratio), -jnp.inf, jnp.float32),
        jnp.zeros((number, groups, ratio), jnp.float32),
        jnp.zeros((number, groups, ratio, HEAD_SIZE), jnp.float32),
    )
    key_piece = lax.all_gather(keys, "ctx", axis=0, tiled=True)
    value_piece = lax.all_gather(values, "ctx", axis=0, tiled=True)
    end_piece = lax.all_gather(subtree_ends, "ctx", axis=0, tiled=True)
    length = key_piece.shape[0]
    step = math.gcd(length, 512)
    turns = length // step

    def single_block(position, state):
        first = position * step
        return block_update(
            state,
            lax.dynamic_slice_in_dim(key_piece, first, step, 0),
            lax.dynamic_slice_in_dim(value_piece, first, step, 0),
            lax.dynamic_slice_in_dim(end_piece, first, step, 0),
            first,
        )

    best, total, summed = lax.fori_loop(0, turns, single_block, initial)
    return (summed / total[..., None]).reshape(number, -1).astype(jnp.bfloat16)


def per_device(queries, keys, values, subtree_ends, query_positions, balance_route, out_weight):
    peers = lax.axis_size("ctx")
    number = queries.shape[0]
    portion = number // peers
    route_row = balance_route[0]
    local = attend(queries, query_positions, keys, values, subtree_ends)
    placed = owner_order(local, route_row).reshape(peers, portion, -1)
    moved = lax.all_to_all(placed, "ctx", split_axis=0, concat_axis=0, tiled=True)
    attended_output = moved.reshape(number, -1)
    return lax.psum_scatter(
        jnp.dot(attended_output, out_weight, preferred_element_type=jnp.float32).astype(
            jnp.bfloat16
        ),
        "tp",
        scatter_dimension=0,
        tiled=True,
    )


def solution(mesh):
    in_specs = (
        P("ctx", "tp"),
        P("ctx", "tp"),
        P("ctx", "tp"),
        P("ctx"),
        P("ctx"),
        P("ctx", None),
        P("tp", None),
    )
    out_specs = P(("ctx", "tp"), None)
    return jax.shard_map(
        per_device, mesh=mesh, in_specs=in_specs, out_specs=out_specs, check_vma=False
    )
```

profile of v0, /device:TPU:1, one launch (start us, length us, event | category | flops | bytes accessed | tf_op | source)
XLA Modules:
  0.0 862.3 jit_solution(3657623575451504358)
XLA Ops:
  13.8 136.8 %all-gather = s32[64,1,256]{2,1,0:T(1,128)S(1)} all-gather(s32[1,1,256]{2,1,0:T(1,128)} %bitcast.68), channel_id=1, replica_groups=mesh['ctx'=64,'tp'=8] {'ctx'}, dimensions={0}, use_global_device_ids=true | all-gather | bytes 66560 | tf_op jit(solution)/shard_map/all_gather | solution.py:66
  150.6 128.6 %all-gather.4.cloned.1.call-done = bf16[16384,128]{1,0:T(8,128)(2,1)} async-done(((bf16[256,128]{1,0:T(8,128)(2,1)}), bf16[16384,128]{1,0:T(8,128)(2,1)}) %all-gather.4.cloned.1.call-update) | async-done | bytes 4194320 | tf_op jit(solution)/shard_map/all_gather | solution.py:64
  279.2 255.9 %all-gather.6.cloned.1.call-done = bf16[16384,128]{0,1:T(8,128)(2,1)} async-done(((bf16[256,128]{0,1:T(8,128)(2,1)}), bf16[16384,128]{0,1:T(8,128)(2,1)}) %all-gather.6.cloned.1.call-update) | async-done | bytes 4194320 | tf_op jit(solution)/shard_map/all_gather | solution.py:65
  535.1 229.6 %while.18 = (s32[]{:T(128)}, f32[128,1,5]{0,2,1:T(8,128)S(1)}, f32[128,1,5]{0,2,1:T(8,128)S(1)}, f32[128,1,5,128]{0,3,2,1:T(8,128)}, s32[128]{0:T(128)}, /*index...) while((s32[]{:T(128)}, f32[128,1,5]{0,2,1:T(8,128)S(1)}, ...), condition=%wide.region_4.5_spmd.clone, body=%wide.region_1.4_spmd.clone.sunk | while | flops 170516480 | bytes 10444523 | solution.py:81
  543.1 2.4 fusion.32
  550.3 2.4 fusion.32
  557.4 2.4 fusion.32
  571.8 2.4 fusion.32
  586.2 2.4 fusion.32
  600.5 2.4 fusion.32
  614.9 2.4 fusion.32
  629.2 2.4 fusion.32
  636.4 2.4 fusion.32
  643.6 2.4 fusion.32
  658.0 2.4 fusion.32
  672.3 2.4 fusion.32
  686.7 2.4 fusion.32
  701.0 2.4 fusion.32
  715.4 2.4 fusion.32
  729.7 2.4 fusion.32
  744.1 2.4 fusion.32
  758.5 2.4 fusion.32
  770.2 16.4 %all_to_all.5 = bf16[64,2,640]{2,1,0:T(2,128)(2,1)} all-to-all(bf16[64,2,640]{2,1,0:T(2,128)(2,1)S(1)} %broadcast_select_fusion), channel_id=1, replica_groups=mesh['ctx'=64,'tp'=8] {'ctx'}, dimensions={0} | all-to-all | bytes 327680 | tf_op jit(solution)/shard_map/all_to_all | solution.py:92
  789.2 66.6 %reduce-scatter.2.cloned.1.call-done = bf16[16,2560]{1,0:T(8,128)(2,1)} async-done(((bf16[128,2560]{1,0:T(8,128)(2,1)}), bf16[16,2560]{1,0:T(8,128)(2,1)}) %reduce-scatter.2.cloned.1.call-update) | async-done | bytes 81936 | tf_op jit(solution)/shard_map/reduce_scatter | solution.py:94
  (394 shorter events, 200.6 us)
Async XLA Ops:
  6.5 781.1 %copy-start = (bf16[640,2560]{1,0:T(8,128)(2,1)S(1)}, bf16[640,2560]{1,0:T(8,128)(2,1)}, u32[]{:S(2)}) copy-start(bf16[640,2560]{1,0:T(8,128)(2,1)} %param.15) | copy-start | bytes 9830404
  6.5 272.7 %all-gather.4.cloned.1.call-start = ((), (), s32[]{:S(2)}) async-start(), calls=%async_computation.2 | async-start | bytes 4259840 | tf_op jit(solution)/shard_map/all_gather | solution.py:64
  7.3 527.9 %all-gather.6.cloned.1.call-start = ((), (), s32[]{:S(2)}) async-start(), calls=%async_computation.3 | async-start | bytes 4259840 | tf_op jit(solution)/shard_map/all_gather | solution.py:65
  9.1 846.7 %reduce-scatter.2.cloned.1.call-start = ((), (), s32[]{:S(2)}) async-start(), calls=%async_computation.4 | async-start | bytes 737280 | tf_op jit(solution)/shard_map/reduce_scatter | solution.py:94
  538.4 1.7 copy-start.1
  545.5 1.7 copy-start.1
  552.7 1.7 copy-start.1
  559.8 1.7 copy-start.1
  567.0 1.7 copy-start.1
  574.2 1.7 copy-start.1
  581.4 1.7 copy-start.1
  588.6 1.7 copy-start.1
  595.7 1.7 copy-start.1
  602.9 1.7 copy-start.1
  610.1 1.7 copy-start.1
  617.3 1.7 copy-start.1
  624.4 1.7 copy-start.1
  631.6 1.7 copy-start.1
  638.8 1.7 copy-start.1
  646.0 1.7 copy-start.1
  653.2 1.7 copy-start.1
  660.3 1.7 copy-start.1
  667.5 1.7 copy-start.1
  674.7 1.7 copy-start.1
  (12 other events, 20.5 us)
Sparse Core Ops, SparseCore 0:
  9.4 269.7 all-gather.3
  281.2 253.8 all-gather.5
  789.3 66.4 reduce-scatter.1
where the time goes:
time: 866 us; the launch traced here: 862 us
  waiting for transfers between devices  452 us (52%)
  blocking collectives  153 us (18%)
  matrix products  146 us (17%)
  other arithmetic  82.1 us (9%)
  local copies, waits for them, and re-layouts  14.4 us (2%)
  between operations  13.2 us (2%)
    all_gather x1, waiting for transfers between devices, attend(): value_piece = lax.all_gather(values, 'ctx', axis=0, tiled=True)  256 us
    all_gather x1, blocking collectives, attend(): end_piece = lax.all_gather(subtree_ends, 'ctx', axis=0, tiled=True)  137 us
    all_gather x1, waiting for transfers between devices, attend(): key_piece = lax.all_gather(keys, 'ctx', axis=0, tiled=True)  129 us
    dot_general x32, matrix products, compute(): jnp.einsum('qgrd,kgd->qgrk', rows, key_block.reshape(width, groups, HEAD_...  76.5 us
    dot_general x32, matrix products, compute(): jnp.einsum('qgrk,kgd->qgrd', weights.astype(jnp.bfloat16), value_block.re...  68.3 us
    reduce_scatter x1, waiting for transfers between devices, per_device(): lax.psum_scatter(jnp.dot(attended_output, out_weight, preferred_element_t...  66.6 us
    reduce_sum x32, other arithmetic, compute(): total = total * factor + jnp.sum(weights, axis=-1)  51.4 us
    and x32, other arithmetic, block_update(): (key_index[None, :] <= query_pos[:, None]) & (query_pos[:, None] < end_bl...  27.3 us
  transfers between devices with their start and end apart: 3, of which 3 were waited for; matrix products, arithmetic and copies ran while one was open for 1% of the time, Pallas kernels for 0%

commit v1 on v0

v1 whole, which is shorter than its diff:
```python
import functools
import math

import jax
import jax.numpy as jnp
from jax import lax
from jax.experimental import pallas as pl
from jax.experimental.pallas import tpu as pltpu
from jax.sharding import PartitionSpec as P

D = 128
HEADS = 5
QW = HEADS * D
NG = 8
NZ = 8
NT = 8
KH = 128
CR = 2 * KH + 16
QR = QW + 16
OW = QW + D
DOUT = 2560
SCALE = math.log2(math.e) / math.sqrt(D)
MASKED = -1e30
START = -1e20
MESH = pl.DeviceIdType.MESH
BF = jnp.bfloat16
F32 = jnp.float32
SPLIT = 3


def digits_row(high, low):
    rows = lax.broadcasted_iota(jnp.int32, (16, D), 0)
    both = jnp.where(rows == 0, jnp.broadcast_to(high, (16, D)), 0)
    both = jnp.where(rows == 1, jnp.broadcast_to(low, (16, D)), both)
    return both.astype(F32).astype(BF)


def kernel(
    q_ref, k_ref, v_ref, i_ref, w_ref, out_ref,
    qt, kv, stage, acc, mx, sm, osend, orecv, att, w_v, part, crecv, ysend, yrecv, zsend, zrecv, fin,
    w_sem, qs, qr, ss, sr, rs, rr, os_, or_, cs, cr, ys, yr, zs, zr,
):
    c, t = lax.axis_index("ctx"), lax.axis_index("tp")
    g, z = c // NZ, c % NZ
    gx, gy = g // 2, g % 2
    th, tc = t // 2, t % 2
    side = g // 4
    low_g = jnp.minimum(g, NG - 1 - g)
    high_g = NG - 1 - low_g
    mate = NG - 1 - g

    def at(group, ring):
        return (group * NZ + ring, t)

    def plane(k):
        step = k // 2
        hop = step + (step // 2) * (1 - 2 * (step % 2))
        return hop, k % 2

    def ahead(k):
        hop, other = plane(k)
        return ((gx + hop) % 4) * 2 + (gy + other) % 2

    def behind(k):
        hop, other = plane(k)
        return ((gx + 4 - hop) % 4) * 2 + (gy + other) % 2

    def remote(src, dst, send, recv, target):
        return pltpu.make_async_remote_copy(
            src_ref=src, dst_ref=dst, send_sem=send, recv_sem=recv, device_id=target, device_id_type=MESH
        )

    w_copy = pltpu.make_async_copy(w_ref, w_v, w_sem)
    w_copy.start()

    barrier = pltpu.get_barrier_semaphore()
    for k in range(1, NG):
        pl.semaphore_signal(barrier, inc=1, device_id=at((g + k) % NG, z), device_id_type=MESH)
    for k in range(1, NZ):
        pl.semaphore_signal(barrier, inc=1, device_id=at(g, (z + k) % NZ), device_id_type=MESH)
    pl.semaphore_signal(barrier, inc=1, device_id=(c, th * 2 + 1 - tc), device_id_type=MESH)
    for k in range(1, 4):
        pl.semaphore_signal(barrier, inc=1, device_id=(c, ((th + k) % 4) * 2 + tc), device_id_type=MESH)

    for half in range(2):
        keys = k_ref[half * KH : (half + 1) * KH, :]
        ends = i_ref[half : half + 1, :]
        ends = digits_row(ends // 128, ends % 128)
        turned = v_ref[half * KH : (half + 1) * KH, :].astype(F32).T.astype(BF)

        def put(ref, keys=keys, ends=ends, turned=turned):
            ref[0:KH, :] = keys
            ref[KH : KH + 16, :] = ends
            ref[KH + 16 :, :] = turned

        @pl.when(side == half)
        def _():
            put(kv.at[side, 0])

        @pl.when(side != half)
        def _():
            put(stage)

    pick = lax.broadcasted_iota(jnp.int32, (D, D), 0) == jnp.broadcast_to(i_ref[3:4, :], (D, D))
    pick = jnp.where(pick, 1.0, 0.0).astype(BF)
    placed = jnp.dot(pick, q_ref[...], preferred_element_type=F32)
    for h in range(HEADS):
        qt[g, h * D : (h + 1) * D, :] = placed[:, h * D : (h + 1) * D].T.astype(BF)
    pos = i_ref[2:3, :]
    pos = digits_row(pos // 128, pos % 128)
    qt[g, QW:, :] = lax.dot_general(pos, pick, (((1,), (1,)), ((), ())), preferred_element_type=F32).astype(BF)

    pl.semaphore_wait(barrier, (NG - 1) + (NZ - 1) + 1 + 3)

    swap = remote(stage, kv.at[side, 0], ss, sr, at(mate, z))
    swap.start()

    right, left = at(g, (z + 1) % NZ), at(g, (z + NZ - 1) % NZ)

    def ring(e, step):
        lane = side if e == 0 else 1 - side
        a, b = (0, 0) if step == 1 else (2 * step - 3, 2 * step - 2)
        if step < 4:
            return (
                remote(kv.at[lane, a], kv.at[lane, 2 * step - 1], rs.at[e, 2 * step - 2], rr.at[e, 2 * step - 2], right),
                remote(kv.at[lane, b], kv.at[lane, 2 * step], rs.at[e, 2 * step - 1], rr.at[e, 2 * step - 1], left),
            )
        cut = KH + 16
        return (
            remote(kv.at[lane, a, 0:cut], kv.at[lane, 7, 0:cut], rs.at[e, 6], rr.at[e, 6], right),
            remote(kv.at[lane, b, cut:CR], kv.at[lane, 7, cut:CR], rs.at[e, 7], rr.at[e, 7], left),
        )

    rings = [[ring(e, step) for step in range(1, 5)] for e in range(2)]

    def launch(e, step):
        if step > 1:
            for copy in rings[e][step - 2]:
                copy.wait_recv()
        elif e == 1:
            swap.wait_recv()
        for copy in rings[e][step - 1]:
            copy.start()

    def query_copy(k):
        return remote(qt.at[g], qt.at[g], qs.at[k], qr.at[k], at(behind(k), z))

    def lower(group):
        return jnp.minimum(group, NG - 1 - group)

    launch(0, 1)
    for k in range(1, NG):

        @pl.when(lower(behind(k)) <= g)
        def _():
            query_copy(k).start()

    launch(1, 1)

    acc[...] = jnp.zeros_like(acc)
    sm[...] = jnp.zeros_like(sm)
    mx[...] = jnp.full_like(mx, START)

    def slot_z(slot):
        hop = (slot + 1) // 2
        return (z + (NZ - hop if slot % 2 else hop)) % NZ

    def flash(b, e, first, last):
        group = low_g if e == 0 else high_g
        row = qt[b, QW : QW + 16, :].astype(F32)
        where = row[0:1, :] * 128.0 + row[1:2, :]
        bias, keys, turned = [], [], []
        for slot in range(first, last):
            ends = kv[e, slot, KH : KH + 16, :].astype(F32)
            ends = jnp.broadcast_to(ends[0:1, :] * 128.0 + ends[1:2, :], (KH, KH)).T
            start = (group * NZ + slot_z(slot)) * (2 * KH) + side * KH
            token = (lax.broadcasted_iota(jnp.int32, (KH, D), 0) + start).astype(F32)
            bias.append(jnp.where((token <= where) & (where < ends), 0.0, MASKED))
            keys.append(kv[e, slot, 0:KH, :])
            turned.append(kv[e, slot, KH + 16 :, :])
        bias, keys, turned = jnp.concatenate(bias, 0), jnp.concatenate(keys, 0), jnp.concatenate(turned, 1)
        for h in range(HEADS):
            cols = slice(h * D, (h + 1) * D)
            s = jnp.dot(keys, qt[b, cols, :], preferred_element_type=F32) + bias
            old = mx[b, 0:1, cols]
            new = jnp.maximum(old, jnp.max(s, axis=0, keepdims=True))
            factor = jnp.exp2((old - new) * SCALE)
            p = jnp.exp2((s - new) * SCALE)
            sm[b, 0:1, cols] = sm[b, 0:1, cols] * factor + jnp.sum(p, axis=0, keepdims=True)
            o = jnp.dot(turned, p.astype(BF), preferred_element_type=F32)
            acc[b, :, cols] = acc[b, :, cols] * factor + o
            mx[b, 0:1, cols] = new

    def first_pass(k, _):
        b = ahead(k)

        @pl.when(b >= low_g)
        def _():
            @pl.when(k > 0)
            def _():
                remote(qt.at[b], qt.at[b], qs.at[k], qr.at[k], at(b, z)).wait_recv()

            flash(b, 0, 0, SPLIT)

        @pl.when(b >= high_g)
        def _():
            flash(b, 1, 0, SPLIT)

        return 0

    launch(0, 2)
    launch(1, 2)
    lax.fori_loop(0, 3, first_pass, 0)
    launch(0, 3)
    launch(1, 3)
    lax.fori_loop(3, 6, first_pass, 0)
    launch(0, 4)
    launch(1, 4)
    lax.fori_loop(6, 8, first_pass, 0)
    for e in range(2):
        for copy in rings[e][3]:
            copy.wait_recv()

    def out_copy(b, k):
        to = (g + k) % NG
        rows = pl.ds(pl.multiple_of(to * 16, 16), 16)
        return remote(osend.at[b, rows], orecv.at[g, b], os_.at[b, k], or_.at[g, b], at(to, z))

    def second_pass(i, _):
        b = NG - 1 - i

        @pl.when(b >= low_g)
        def _():
            flash(b, 0, SPLIT, NZ)

        @pl.when(b >= high_g)
        def _():
            flash(b, 1, SPLIT, NZ)

        @pl.when(b >= low_g)
        def _():
            stats = []
            for h in range(HEADS):
                cols = slice(h * D, (h + 1) * D)
                total = sm[b, 0:1, cols]
                some = total > 0.0
                safe = jnp.where(some, total, 1.0)
                osend[b, :, cols] = (acc[b, :, cols] / safe).T.astype(BF)
                stats.append(jnp.where(some, mx[b, 0:1, cols] * SCALE + jnp.log2(safe), START))
            lse = jnp.concatenate(stats + [jnp.zeros((8 - HEADS, D), F32)], 0)
            one = lse.astype(BF).astype(F32)
            two = (lse - one).astype(BF).astype(F32)
            three = lse - one - two
            table = jnp.concatenate([one, two, three, jnp.zeros((D - 24, D), F32)], 0)
            osend[b, :, QW:] = table.T.astype(BF)
            for k in range(1, NG):
                out_copy(b, k).start()
            orecv[g, b] = osend[b, pl.ds(pl.multiple_of(g * 16, 16), 16), :]

        return 0

    lax.fori_loop(0, NG, second_pass, 0)

    for b in range(NG):
        sources = [s for s in range(NG) if min(s, NG - 1 - s) <= b]
        lses = []
        for s in sources:

            @pl.when(g != s)
            def _():
                remote(orecv.at[s, b], orecv.at[s, b], os_.at[b, 0], or_.at[s, b], at(s, z)).wait_recv()

            digits = orecv[s, b, :, QW:].astype(F32)
            lses.append(digits + pltpu.roll(digits, D - 8, 1) + pltpu.roll(digits, D - 16, 1))
        best = functools.reduce(jnp.maximum, lses)
        weights = [jnp.exp2(lse - best) for lse in lses]
        total = functools.reduce(jnp.add, weights)
        weights = [w / total for w in weights]
        for h in range(HEADS):
            cols = slice(h * D, (h + 1) * D)
            mixed = jnp.zeros((16, D), F32)
            for s, w in zip(sources, weights):
                mixed = mixed + orecv[s, b, :, cols].astype(F32) * w[:, h : h + 1]
            att[b * 16 : (b + 1) * 16, cols] = mixed.astype(BF)

    w_copy.wait()
    for n in range(DOUT // 512):
        cols = slice(n * 512, (n + 1) * 512)
        part[:, cols] = jnp.dot(att[...], w_v[:, cols], preferred_element_type=F32).astype(BF)

    def rows_of(high, core):
        return pl.ds(pl.multiple_of((high * 2 + core) * 16, 16), 16)

    core = [
        remote(part.at[rows_of(j, 1 - tc)], crecv.at[j], cs.at[j], cr.at[j], (c, th * 2 + 1 - tc)) for j in range(4)
    ]
    for copy in core:
        copy.start()
    along = []
    for j in range(4):
        core[j].wait_recv()
        both = part[rows_of(j, tc), :].astype(F32) + crecv[j].astype(F32)

        ysend[j] = both.astype(BF)

        def across(j=j):
            return remote(ysend.at[j], yrecv.at[th], ys.at[j], yr.at[th], (c, j * 2 + tc))

        along.append(across)

        @pl.when(th != j)
        def _():
            across().start()

        @pl.when(th == j)
        def _():
            yrecv[th] = both.astype(BF)

    for j in range(4):

        @pl.when(th != j)
        def _():
            remote(yrecv.at[j], yrecv.at[j], ys.at[j], yr.at[j], (c, j * 2 + tc)).wait_recv()

    total = yrecv[0].astype(F32) + yrecv[1].astype(F32) + yrecv[2].astype(F32) + yrecv[3].astype(F32)
    fin[...] = total
    for j in range(NZ):
        zsend[j] = fin[2 * j : 2 * j + 2, :]
    last = []
    for k in range(1, NZ):
        to = (z + k) % NZ
        copy = remote(zsend.at[to], zrecv.at[z], zs.at[k], zr.at[k], at(g, to))
        copy.start()
        last.append(copy)
    zrecv[z] = zsend[z]
    for copy in last:
        copy.wait_recv()
    for j in range(NZ):
        fin[2 * j : 2 * j + 2, :] = zrecv[j]
    out_ref[...] = fin[...].astype(BF)

    swap.wait_send()
    for e in range(2):
        for pair in rings[e]:
            for copy in pair:
                copy.wait_send()
    for k in range(1, NG):

        @pl.when(lower(behind(k)) <= g)
        def _():
            query_copy(k).wait_send()

    for b in range(NG):

        @pl.when(b >= low_g)
        def _():
            for k in range(1, NG):
                out_copy(b, k).wait_send()

    for copy in core:
        copy.wait_send()
    for j in range(4):

        @pl.when(th != j)
        def _():
            along[j]().wait_send()

    for copy in last:
        copy.wait_send()


def per_device(queries, keys, values, subtree_ends, query_positions, balance_route, out_weight):
    small = jnp.concatenate(
        [
            subtree_ends.reshape(2, D),
            query_positions.reshape(1, D),
            balance_route.reshape(1, D),
            jnp.zeros((4, D), jnp.int32),
        ],
        axis=0,
    )
    vmem = pl.BlockSpec(memory_space=pltpu.VMEM)
    dma = pltpu.SemaphoreType.DMA
    return pl.pallas_call(
        kernel,
        out_shape=jax.ShapeDtypeStruct((16, DOUT), BF),
        in_specs=[vmem, vmem, vmem, vmem, pl.BlockSpec(memory_space=pl.ANY)],
        out_specs=vmem,
        scratch_shapes=[
            pltpu.VMEM((NG, QR, D), BF),
            pltpu.VMEM((2, NZ, CR, D), BF),
            pltpu.VMEM((CR, D), BF),
            pltpu.VMEM((NG, D, QW), F32),
            pltpu.VMEM((NG, 8, QW), F32),
            pltpu.VMEM((NG, 8, QW), F32),
            pltpu.VMEM((NG, D, OW), BF),
            pltpu.VMEM((NG, NG, 16, OW), BF),
            pltpu.VMEM((D, QW), BF),
            pltpu.VMEM((QW, DOUT), BF),
            pltpu.VMEM((D, DOUT), BF),
            pltpu.VMEM((4, 16, DOUT), BF),
            pltpu.VMEM((4, 16, DOUT), BF),
            pltpu.VMEM((4, 16, DOUT), BF),
            pltpu.VMEM((NZ, 2, DOUT), F32),
            pltpu.VMEM((NZ, 2, DOUT), F32),
            pltpu.VMEM((16, DOUT), F32),
            dma,
            dma((NG,)), dma((NG,)),
            dma, dma,
            dma((2, 8)), dma((2, 8)),
            dma((NG, NG)), dma((NG, NG)),
            dma((4,)), dma((4,)),
            dma((4,)), dma((4,)),
            dma((NZ,)), dma((NZ,)),
        ],
        compiler_params=pltpu.CompilerParams(
            collective_id=0, has_side_effects=True, vmem_limit_bytes=48 << 20
        ),
        name="tree_attention",
    )(queries, keys, values, small, out_weight)


def solution(mesh):
    in_specs = (
        P("ctx", "tp"),
        P("ctx", "tp"),
        P("ctx", "tp"),
        P("ctx"),
        P("ctx"),
        P("ctx", None),
        P("tp", None),
    )
    out_specs = P(("ctx", "tp"), None)
    return jax.shard_map(
        per_device, mesh=mesh, in_specs=in_specs, out_specs=out_specs, check_vma=False
    )
```

time: 866 us -> 90.1 us (0.10)
  waiting for transfers between devices: 452 us -> 0 us
  blocking collectives: 153 us -> 0 us
  matrix products: 146 us -> 0 us
  Pallas kernels: 0 us -> 83.4 us
  other arithmetic: 82.1 us -> 0.78 us
  between operations: 13.2 us -> 0.01 us
  local copies, waits for them, and re-layouts: 14.4 us -> 5.24 us
    all_gather x2 -> x0, waiting for transfers between devices: 385 us -> none  [the longest x1 256 us: attend(): value_piece = lax.all_gather(values, 'ctx', axis=0, tiled=True)]
    dot_general x65 -> x0, matrix products: 146 us -> none  [the longest x32 76.5 us: compute(): jnp.einsum('qgrd,kgd->qgrk', rows, key_block.reshape(width, groups, HEAD_...]
    all_gather x1 -> x0, blocking collectives: 137 us -> none  [attend(): end_piece = lax.all_gather(subtree_ends, 'ctx', axis=0, tiled=True)]
    pallas_call x0 -> x1, Pallas kernels: none -> 83.4 us  [per_device(): pl.pallas_call(kernel, out_shape=jax.ShapeDtypeStruct((16, DOUT), BF), in...]
    reduce_scatter x1 -> x0, waiting for transfers between devices: 66.6 us -> none  [per_device(): lax.psum_scatter(jnp.dot(attended_output, out_weight, preferred_element_t...]
    reduce_sum x32 -> x0, other arithmetic: 51.4 us -> none  [compute(): total = total * factor + jnp.sum(weights, axis=-1)]
    and x33 -> x0, other arithmetic: 27.3 us -> none  [the longest x32 27.3 us: block_update(): (key_index[None, :] <= query_pos[:, None]) & (query_pos[:, None] < end_bl...]
    all_to_all x1 -> x0, blocking collectives: 16.4 us -> none  [per_device(): lax.all_to_all(placed, 'ctx', split_axis=0, concat_axis=0, tiled=True)]
  transfers between devices with their start and end apart: 3 -> 0, of which waited for: 3 -> 0; matrix products, arithmetic and copies ran while one was open for 1% -> 0% of each run, Pallas kernels for 0% -> 0%
where the time goes in v1:
time: 90.1 us; the launch traced here: 89.4 us
  Pallas kernels  83.4 us (93%)
  local copies, waits for them, and re-layouts  5.24 us (6%)
    pallas_call x1, Pallas kernels, per_device(): pl.pallas_call(kernel, out_shape=jax.ShapeDtypeStruct((16, DOUT), BF), in...  83.4 us
    unnamed x9, local copies, waits for them, and re-layouts  5.16 us

profile of v1, /device:TPU:1, one launch (start us, length us, event | category | flops | bytes accessed | tf_op | source)
XLA Modules:
  0.0 89.4 jit_solution(625955803706247383)
XLA Ops:
  0.0 0.1 pad.3.clone
  0.1 0.8 add_add_fusion.i_ref
  0.9 0.0 copy-start
  0.9 1.9 %copy-done = bf16[640,2560]{1,0:T(8,128)(2,1)S(1)} copy-done((bf16[640,2560]{1,0:T(8,128)(2,1)S(1)}, bf16[640,2560]{1,0:T(8,128)(2,1)}, u32[]{:S(2)}) %copy-start) | copy-done | bytes 3276824
  2.8 0.0 copy-start.1
  2.8 0.9 %copy-done.1 = bf16[128,640]{1,0:T(8,128)(2,1)S(1)} copy-done((bf16[128,640]{1,0:T(8,128)(2,1)S(1)}, bf16[128,640]{1,0:T(8,128)(2,1)}, u32[]{:S(2)}) %copy-start.1) | copy-done | bytes 163864
  3.7 0.0 copy-start.2
  3.7 0.8 copy-done.2
  4.5 0.0 copy-start.3
  4.5 0.8 copy-done.3
  5.4 83.4 %tree_attention.1 = bf16[16,2560]{1,0:T(8,128)(2,1)S(1)} custom-call(bf16[128,640]{1,0:T(8,128)(2,1)S(1)} %copy-done.1, bf16[256,128]{1,0:T(8,128)(2,1)S(1)} %copy-done.2, bf16[256,128]{1,0:T(8,128)(2,1)S(1)} %copy-done.3, s32[8,128]{1,0:T(8,128)S(1)} %add_add_fusion.i_ref, bf16[640,2560]{1,0:T(8,128)(2,1)S(1)} %copy-done), custom_call_target="tpu_custom_call" | custom-call | tf_op jit(solution)/shard_map/tree_attention/pallas_call | solution.py:384
  88.8 0.6 copy.9
  (1 shorter events, 0.0 us)
Async XLA Ops:
  0.9 1.9 %copy-start = (bf16[640,2560]{1,0:T(8,128)(2,1)S(1)}, bf16[640,2560]{1,0:T(8,128)(2,1)}, u32[]{:S(2)}) copy-start(bf16[640,2560]{1,0:T(8,128)(2,1)} %w_ref.1) | copy-start | bytes 9830404
  2.8 0.9 %copy-start.1 = (bf16[128,640]{1,0:T(8,128)(2,1)S(1)}, bf16[128,640]{1,0:T(8,128)(2,1)}, u32[]{:S(2)}) copy-start(bf16[128,640]{1,0:T(8,128)(2,1)} %q_ref.1) | copy-start | bytes 491524
  3.7 0.8 copy-start.2
  4.5 0.8 copy-start.3

commit v2 on v1

v2 whole, which is shorter than its diff:
```python
import functools
import math

import jax
import jax.numpy as jnp
from jax import lax
from jax.experimental import pallas as pl
from jax.experimental.pallas import tpu as pltpu
from jax.sharding import PartitionSpec as P

D = 128
HEADS = 5
QW = HEADS * D
NX, NY, NZ = 4, 2, 8
NG = NX * NY
KH = 128
CUT = KH + 16
CR = CUT + KH
QR = QW + 16
OW = QW + D
DOUT = 2560
SCALE = math.log2(math.e) / math.sqrt(D)
MASKED = -1e30
START = -1e20
MESH = pl.DeviceIdType.MESH
BF = jnp.bfloat16
F32 = jnp.float32


def digits_row(high, low):
    rows = lax.broadcasted_iota(jnp.int32, (16, D), 0)
    both = jnp.where(rows == 0, jnp.broadcast_to(high, (16, D)), 0)
    both = jnp.where(rows == 1, jnp.broadcast_to(low, (16, D)), both)
    return both.astype(F32).astype(BF)


def kernel(
    q_in, k_in, v_in, e_in, p_in, r_in, w_in, out_ref,
    q_ref, k_ref, v_ref, e_ref, p_ref, r_ref,
    qt, kv, ends, stage, acc, mx, sm, osend, orecv, att, w_v, part, crecv, ysend, yrecv, zsend, zrecv, fin,
    in_sem, w_sem, qs, qr, ss, sr, rs, rr, ns, nr, os_, or_, cs, cr, ys, yr, zs, zr,
):
    c, t = lax.axis_index("ctx"), lax.axis_index("tp")
    x, y, z = c // (NY * NZ), (c // NZ) % NY, c % NZ
    g = c // NZ
    th, tc = t // 2, t % 2
    side = x // 2
    low_x = jnp.minimum(x, NX - 1 - x)
    high_x = NX - 1 - low_x

    def at(group, ring):
        return (group * NZ + ring, t)

    def remote(src, dst, send, recv, target):
        return pltpu.make_async_remote_copy(
            src_ref=src, dst_ref=dst, send_sem=send, recv_sem=recv, device_id=target, device_id_type=MESH
        )

    pairs = ((e_in, e_ref), (k_in, k_ref), (v_in, v_ref), (r_in, r_ref), (q_in, q_ref), (p_in, p_ref))
    loads = [pltpu.make_async_copy(src, dst, in_sem.at[n]) for n, (src, dst) in enumerate(pairs)]
    for load in loads:
        load.start()
    w_copy = pltpu.make_async_copy(w_in, w_v, w_sem)
    w_copy.start()

    barrier = pltpu.get_barrier_semaphore()
    for k in range(1, NG):
        pl.semaphore_signal(barrier, inc=1, device_id=at((g + k) % NG, z), device_id_type=MESH)
    for k in range(1, NZ):
        pl.semaphore_signal(barrier, inc=1, device_id=at(g, (z + k) % NZ), device_id_type=MESH)
    pl.semaphore_signal(barrier, inc=1, device_id=(c, th * 2 + 1 - tc), device_id_type=MESH)
    for k in range(1, 4):
        pl.semaphore_signal(barrier, inc=1, device_id=(c, ((th + k) % 4) * 2 + tc), device_id_type=MESH)

    for load in loads[:3]:
        load.wait()
    for half in range(2):
        keys = k_ref[half * KH : (half + 1) * KH, :]
        last_tokens = e_ref[half : half + 1, :]
        last_tokens = digits_row(last_tokens // 128, last_tokens % 128)
        turned = v_ref[half * KH : (half + 1) * KH, :].astype(F32).T.astype(BF)

        def put(ref, keys=keys, last_tokens=last_tokens, turned=turned):
            ref[0:KH, :] = keys
            ref[KH:CUT, :] = last_tokens
            ref[CUT:, :] = turned

        @pl.when(side == half)
        def _():
            put(kv.at[side, 0])

        @pl.when(side != half)
        def _():
            put(stage)

    for load in loads[3:]:
        load.wait()
    pick = lax.broadcasted_iota(jnp.int32, (D, D), 0) == jnp.broadcast_to(r_ref[...], (D, D))
    pick = jnp.where(pick, 1.0, 0.0).astype(BF)
    placed = jnp.dot(pick, q_ref[...], preferred_element_type=F32)
    for h in range(HEADS):
        qt[x, h * D : (h + 1) * D, :] = placed[:, h * D : (h + 1) * D].T.astype(BF)
    pos = p_ref[...]
    pos = digits_row(pos // 128, pos % 128)
    qt[x, QW:, :] = lax.dot_general(pos, pick, (((1,), (1,)), ((), ())), preferred_element_type=F32).astype(BF)

    pl.semaphore_wait(barrier, (NG - 1) + (NZ - 1) + 1 + 3)

    swap = remote(stage, kv.at[side, 0], ss, sr, at((NX - 1 - x) * NY + y, z))
    swap.start()

    right, left, beside = at(g, (z + 1) % NZ), at(g, (z + NZ - 1) % NZ), at(x * NY + 1 - y, z)

    def ring(e, r, step):
        lane = side if e == 0 else 1 - side
        a, b = (0, 0) if step == 1 else (2 * step - 3, 2 * step - 2)
        a, b = 2 * a + r, 2 * b + r
        n = 2 * step - 2
        sem = lambda sems, m: sems.at[e * 16 + r * 8 + m]
        if step < 4:
            to = 2 * (n + 1) + r
            return (
                remote(kv.at[lane, a], kv.at[lane, to], sem(rs, n), sem(rr, n), right),
                remote(kv.at[lane, b], kv.at[lane, to + 2], sem(rs, n + 1), sem(rr, n + 1), left),
            )
        to = 14 + r
        return (
            remote(kv.at[lane, a, 0:CUT], kv.at[lane, to, 0:CUT], sem(rs, 6), sem(rr, 6), right),
            remote(kv.at[lane, b, CUT:CR], kv.at[lane, to, CUT:CR], sem(rs, 7), sem(rr, 7), left),
        )

    def next_row(e, i):
        lane = side if e == 0 else 1 - side
        return remote(kv.at[lane, 2 * i], kv.at[lane, 2 * i + 1], ns.at[e * 3 + i], nr.at[e * 3 + i], beside)

    rings = [[{s: ring(e, r, s) for s in range(1 + r, 5)} for r in range(2)] for e in range(2)]
    sides = [[next_row(e, i) for i in range(3)] for e in range(2)]

    def launch_first(e):
        if e == 1:
            swap.wait_recv()
        for copy in rings[e][0][1]:
            copy.start()
        sides[e][0].start()

    def launch_second(e):
        for i, copy in enumerate(rings[e][0][1]):
            copy.wait_recv()
            rings[e][0][2][i].start()
            sides[e][1 + i].start()

    def launch_second_other(e):
        for i in range(2):
            sides[e][1 + i].wait_recv()
            rings[e][1][2][i].start()

    def launch_later(e, r, step):
        for i, copy in enumerate(rings[e][r][step - 1]):
            copy.wait_recv()
        for copy in rings[e][r][step]:
            copy.start()

    def query_copy(k):
        return remote(qt.at[x], qt.at[x], qs.at[k], qr.at[k], at(((x + NX - k) % NX) * NY + y, z))

    def wanted(k):
        to = (x + NX - k) % NX
        return jnp.minimum(to, NX - 1 - to) <= x

    launch_first(0)
    for k in (1, 3, 2):

        @pl.when(wanted(k))
        def _():
            query_copy(k).start()

    launch_first(1)

    acc[...] = jnp.zeros_like(acc)
    sm[...] = jnp.zeros_like(sm)
    mx[...] = jnp.full_like(mx, START)

    def slot_start(e, slot):
        i, r = slot // 2, slot % 2
        hop = (i + 1) // 2
        ring_at = (z + (NZ - hop if i % 2 else hop)) % NZ
        row = y if r == 0 else 1 - y
        group = low_x if e == 0 else high_x
        return ((group * NY + row) * NZ + ring_at) * (2 * KH) + side * KH

    def turn_ends(first, last):
        for e in range(2):
            for slot in range(first, last):
                row = kv[e, slot, KH:CUT, :].astype(F32)
                ends[e, slot] = jnp.broadcast_to(row[0:1, :] * 128.0 + row[1:2, :], (KH, KH)).T

    def flash(b, e, first, last):
        row = qt[b, QW : QW + 16, :].astype(F32)
        where = row[0:1, :] * 128.0 + row[1:2, :]
        bias, keys, turned = [], [], []
        for slot in range(first, last):
            token = (lax.broadcasted_iota(jnp.int32, (KH, D), 0) + slot_start(e, slot)).astype(F32)
            bias.append(jnp.where((token <= where) & (where < ends[e, slot]), 0.0, MASKED))
            keys.append(kv[e, slot, 0:KH, :])
            turned.append(kv[e, slot, CUT:, :])
        bias, keys, turned = jnp.concatenate(bias, 0), jnp.concatenate(keys, 0), jnp.concatenate(turned, 1)
        for h in range(HEADS):
            cols = slice(h * D, (h + 1) * D)
            s = jnp.dot(keys, qt[b, cols, :], preferred_element_type=F32) + bias
            old = mx[b, 0:1, cols]
            new = jnp.maximum(old, jnp.max(s, axis=0, keepdims=True))
            factor = jnp.exp2((old - new) * SCALE)
            p = jnp.exp2((s - new) * SCALE)
            sm[b, 0:1, cols] = sm[b, 0:1, cols] * factor + jnp.sum(p, axis=0, keepdims=True)
            o = jnp.dot(turned, p.astype(BF), preferred_element_type=F32)
            acc[b, :, cols] = acc[b, :, cols] * factor + o
            mx[b, 0:1, cols] = new

    def first_pass(n, _):
        k = n + (n // 2) * (1 - 2 * (n % 2))
        b = (x + k) % NX

        @pl.when(b >= low_x)
        def _():
            @pl.when(k > 0)
            def _():
                remote(qt.at[b], qt.at[b], qs.at[k], qr.at[k], at(b * NY + y, z)).wait_recv()

            flash(b, 0, 0, 6)

        @pl.when(b >= high_x)
        def _():
            flash(b, 1, 0, 6)

        return 0

    def middle_pass(n, _):
        b = NX - 1 - n

        @pl.when(b >= low_x)
        def _():
            flash(b, 0, 6, 10)

        @pl.when(b >= high_x)
        def _():
            flash(b, 1, 6, 10)

        return 0

    launch_second(0)
    launch_second(1)
    for e in range(2):
        sides[e][0].wait_recv()
    launch_second_other(0)
    launch_second_other(1)
    turn_ends(0, 6)
    lax.fori_loop(0, 2, first_pass, 0)
    for e in range(2):
        for r in range(2):
            launch_later(e, r, 3)
    turn_ends(6, 10)
    lax.fori_loop(2, 4, first_pass, 0)
    for e in range(2):
        for r in range(2):
            launch_later(e, r, 4)
    lax.fori_loop(0, NX, middle_pass, 0)
    for e in range(2):
        for r in range(2):
            for copy in rings[e][r][4]:
                copy.wait_recv()
    turn_ends(10, 16)

    def out_copy(b, k):
        to = (g + k) % NG
        rows = pl.ds(pl.multiple_of(to * 16, 16), 16)
        return remote(
            osend.at[b, rows], orecv.at[x, b * NY + y], os_.at[b * NG + k], or_.at[x * NG + b * NY + y], at(to, z)
        )

    def last_pass(n, _):
        b = NX - 1 - n

        @pl.when(b >= low_x)
        def _():
            flash(b, 0, 10, 16)

        @pl.when(b >= high_x)
        def _():
            flash(b, 1, 10, 16)

        @pl.when(b >= low_x)
        def _():
            stats = []
            for h in range(HEADS):
                cols = slice(h * D, (h + 1) * D)
                total = sm[b, 0:1, cols]
                some = total > 0.0
                safe = jnp.where(some, total, 1.0)
                osend[b, :, cols] = (acc[b, :, cols] / safe).T.astype(BF)
                stats.append(jnp.where(some, mx[b, 0:1, cols] * SCALE + jnp.log2(safe), START))
            lse = jnp.concatenate(stats + [jnp.zeros((8 - HEADS, D), F32)], 0)
            one = lse.astype(BF).astype(F32)
            two = (lse - one).astype(BF).astype(F32)
            three = lse - one - two
            table = jnp.concatenate([one, two, three, jnp.zeros((D - 24, D), F32)], 0)
            osend[b, :, QW:] = table.T.astype(BF)
            for k in range(1, NG):
                out_copy(b, k).start()
            orecv[x, b * NY + y] = osend[b, pl.ds(pl.multiple_of(g * 16, 16), 16), :]

        return 0

    lax.fori_loop(0, NX, last_pass, 0)

    lanes = lax.broadcasted_iota(jnp.int32, (D, QW), 0)
    heads = lax.broadcasted_iota(jnp.int32, (D, QW), 1) // D
    spread = jnp.where((lanes == heads) | (lanes == heads + 8), 1.0, 0.0).astype(BF)
    used = lax.broadcasted_iota(jnp.int32, (16, D), 1) < 8
    for b in reversed(range(NG)):
        sources = [s for s in range(NX) if min(s, NX - 1 - s) <= b // NY]
        lses = []
        for s in sources:

            @pl.when((x != s) | (y != b % NY))
            def _():
                remote(
                    orecv.at[s, b], orecv.at[s, b], os_.at[b], or_.at[s * NG + b], at(s * NY + b % NY, z)
                ).wait_recv()

            digits = orecv[s, b, :, QW:].astype(F32)
            lses.append(digits + pltpu.roll(digits, D - 8, 1) + pltpu.roll(digits, D - 16, 1))
        best = functools.reduce(jnp.maximum, lses)
        weights = [jnp.exp2(lse - best) for lse in lses]
        total = functools.reduce(jnp.add, weights)
        rows = []
        for w in weights:
            w = w / total
            high = w.astype(BF).astype(F32)
            rows.append(jnp.where(used, high, pltpu.roll(w - high, 8, 1)).astype(BF))
        wide = jnp.dot(jnp.concatenate(rows, 0), spread, preferred_element_type=F32)
        mixed = jnp.zeros((16, QW), F32)
        for n, s in enumerate(sources):
            mixed = mixed + orecv[s, b, :, 0:QW].astype(F32) * wide[n * 16 : (n + 1) * 16, :]
        att[b * 16 : (b + 1) * 16, :] = mixed.astype(BF)

    w_copy.wait()
    for n in range(DOUT // 512):
        cols = slice(n * 512, (n + 1) * 512)
        part[:, cols] = jnp.dot(att[...], w_v[:, cols], preferred_element_type=F32).astype(BF)

    def rows_of(high, core):
        return pl.ds(pl.multiple_of((high * 2 + core) * 16, 16), 16)

    core = [
        remote(part.at[rows_of(j, 1 - tc)], crecv.at[j], cs.at[j], cr.at[j], (c, th * 2 + 1 - tc)) for j in range(4)
    ]
    for copy in core:
        copy.start()
    along = []
    for j in range(4):
        core[j].wait_recv()
        both = part[rows_of(j, tc), :].astype(F32) + crecv[j].astype(F32)

        ysend[j] = both.astype(BF)

        def across(j=j):
            return remote(ysend.at[j], yrecv.at[th], ys.at[j], yr.at[th], (c, j * 2 + tc))

        along.append(across)

        @pl.when(th != j)
        def _():
            across().start()

        @pl.when(th == j)
        def _():
            yrecv[th] = both.astype(BF)

    for j in range(4):

        @pl.when(th != j)
        def _():
            remote(yrecv.at[j], yrecv.at[j], ys.at[j], yr.at[j], (c, j * 2 + tc)).wait_recv()

    total = yrecv[0].astype(F32) + yrecv[1].astype(F32) + yrecv[2].astype(F32) + yrecv[3].astype(F32)
    fin[...] = total
    for j in range(NZ):
        zsend[j] = fin[2 * j : 2 * j + 2, :]
    last = []
    for k in range(1, NZ):
        to = (z + k) % NZ
        copy = remote(zsend.at[to], zrecv.at[z], zs.at[k], zr.at[k], at(g, to))
        copy.start()
        last.append(copy)
    zrecv[z] = zsend[z]
    for copy in last:
        copy.wait_recv()
    for j in range(NZ):
        fin[2 * j : 2 * j + 2, :] = zrecv[j]
    out_ref[...] = fin[...].astype(BF)

    swap.wait_send()
    for e in range(2):
        for copy in sides[e]:
            copy.wait_send()
        for r in range(2):
            for pair in rings[e][r].values():
                for copy in pair:
                    copy.wait_send()
    for k in range(1, NX):

        @pl.when(wanted(k))
        def _():
            query_copy(k).wait_send()

    for b in range(NX):

        @pl.when(b >= low_x)
        def _():
            for k in range(1, NG):
                out_copy(b, k).wait_send()

    for copy in core:
        copy.wait_send()
    for j in range(4):

        @pl.when(th != j)
        def _():
            along[j]().wait_send()

    for copy in last:
        copy.wait_send()


def per_device(queries, keys, values, subtree_ends, query_positions, balance_route, out_weight):
    dma = pltpu.SemaphoreType.DMA
    return pl.pallas_call(
        kernel,
        out_shape=jax.ShapeDtypeStruct((16, DOUT), BF),
        in_specs=[pl.BlockSpec(memory_space=pltpu.HBM)] * 7,
        out_specs=pl.BlockSpec(memory_space=pltpu.VMEM),
        scratch_shapes=[
            pltpu.VMEM((D, QW), BF),
            pltpu.VMEM((2 * KH, D), BF),
            pltpu.VMEM((2 * KH, D), BF),
            pltpu.VMEM((2, D), jnp.int32),
            pltpu.VMEM((1, D), jnp.int32),
            pltpu.VMEM((1, D), jnp.int32),
            pltpu.VMEM((NX, QR, D), BF),
            pltpu.VMEM((2, 2 * NZ, CR, D), BF),
            pltpu.VMEM((2, 2 * NZ, KH, KH), F32),
            pltpu.VMEM((CR, D), BF),
            pltpu.VMEM((NX, D, QW), F32),
            pltpu.VMEM((NX, 8, QW), F32),
            pltpu.VMEM((NX, 8, QW), F32),
            pltpu.VMEM((NX, D, OW), BF),
            pltpu.VMEM((NX, NG, 16, OW), BF),
            pltpu.VMEM((D, QW), BF),
            pltpu.VMEM((QW, DOUT), BF),
            pltpu.VMEM((D, DOUT), BF),
            pltpu.VMEM((4, 16, DOUT), BF),
            pltpu.VMEM((4, 16, DOUT), BF),
            pltpu.VMEM((4, 16, DOUT), BF),
            pltpu.VMEM((NZ, 2, DOUT), F32),
            pltpu.VMEM((NZ, 2, DOUT), F32),
            pltpu.VMEM((16, DOUT), F32),
            dma((6,)), dma,
            dma((NX,)), dma((NX,)),
            dma, dma,
            dma((32,)), dma((32,)),
            dma((6,)), dma((6,)),
            dma((NX * NG,)), dma((NX * NG,)),
            dma((4,)), dma((4,)),
            dma((4,)), dma((4,)),
            dma((NZ,)), dma((NZ,)),
        ],
        compiler_params=pltpu.CompilerParams(
            collective_id=0, has_side_effects=True, vmem_limit_bytes=56 << 20
        ),
        name="tree_attention",
    )(
        queries, keys, values, subtree_ends.reshape(2, D), query_positions.reshape(1, D), balance_route.reshape(1, D),
        out_weight,
    )


def solution(mesh):
    in_specs = (
        P("ctx", "tp"),
        P("ctx", "tp"),
        P("ctx", "tp"),
        P("ctx"),
        P("ctx"),
        P("ctx", None),
        P("tp", None),
    )
    out_specs = P(("ctx", "tp"), None)
    return jax.shard_map(
        per_device, mesh=mesh, in_specs=in_specs, out_specs=out_specs, check_vma=False
    )
```

time: 90.1 us -> 75.6 us (0.84)
  Pallas kernels: 83.4 us -> 73 us
  local copies, waits for them, and re-layouts: 5.24 us -> 1.53 us
    pallas_call x1, Pallas kernels: 83.4 us -> 73 us  [per_device(): pl.pallas_call(kernel, out_shape=jax.ShapeDtypeStruct((16, DOUT), BF), in...]
    unnamed x9 -> x1, local copies, waits for them, and re-layouts: 5.16 us -> 1.53 us
where the time goes in v2:
time: 75.6 us; the launch traced here: 74.5 us
  Pallas kernels  73 us (97%)
  local copies, waits for them, and re-layouts  1.53 us (2%)
    pallas_call x1, Pallas kernels, per_device(): pl.pallas_call(kernel, out_shape=jax.ShapeDtypeStruct((16, DOUT), BF), in...  73 us
    unnamed x1, local copies, waits for them, and re-layouts  1.53 us

profile of v2, /device:TPU:1, one launch (start us, length us, event | category | flops | bytes accessed | tf_op | source)
XLA Modules:
  0.0 74.5 jit_solution(11189856690601159667)
XLA Ops:
  0.0 73.0 %tree_attention.1 = bf16[16,2560]{1,0:T(8,128)(2,1)} custom-call(bf16[128,640]{1,0:T(8,128)(2,1)} %q_in.1, bf16[256,128]{1,0:T(8,128)(2,1)} %k_in.1, bf16[256,128]{1,0:T(8,128)(2,1)} %v_in.1, s32[2,128]{1,0:T(2,128)} %bitcast.2, s32[1,128]{1,0:T(1,128)} %bitcast.3, s32[1,128]{1,0:T(1,128)} %r_in.1, bf16[640,2560]{1,0:T(8,128)(2,1)} %w_in.1), custom_call_target="tpu_custom_call" | custom-call | tf_op jit(solution)/shard_map/tree_attention/pallas_call | solution.py:437
  73.0 1.5 %copy.9 = bf16[16,2560]{1,0:T(8,128)(2,1)} copy(bf16[16,2560]{1,0:T(8,128)(2,1)} %tree_attention.1) | data formatting | bytes 163840

commit v3 on v2

--- a/solution.py
+++ b/solution.py
@@ -37,7 +37,7 @@
 def kernel(
     q_in, k_in, v_in, e_in, p_in, r_in, w_in, out_ref,
     q_ref, k_ref, v_ref, e_ref, p_ref, r_ref,
-    qt, kv, ends, stage, acc, mx, sm, osend, orecv, att, w_v, part, crecv, ysend, yrecv, zsend, zrecv, fin,
+    qz_out, qz, qt, kv, ends, stage, acc, mx, sm, osend, orecv, att, w_v, part, crecv, ysend, yall,
     in_sem, w_sem, qs, qr, ss, sr, rs, rr, ns, nr, os_, or_, cs, cr, ys, yr, zs, zr,
 ):
     c, t = lax.axis_index("ctx"), lax.axis_index("tp")
@@ -61,7 +61,6 @@
     for load in loads:
         load.start()
     w_copy = pltpu.make_async_copy(w_in, w_v, w_sem)
-    w_copy.start()
 
     barrier = pltpu.get_barrier_semaphore()
     for k in range(1, NG):
@@ -92,17 +91,6 @@
         @pl.when(side != half)
         def _():
             put(stage)
-
-    for load in loads[3:]:
-        load.wait()
-    pick = lax.broadcasted_iota(jnp.int32, (D, D), 0) == jnp.broadcast_to(r_ref[...], (D, D))
-    pick = jnp.where(pick, 1.0, 0.0).astype(BF)
-    placed = jnp.dot(pick, q_ref[...], preferred_element_type=F32)
-    for h in range(HEADS):
-        qt[x, h * D : (h + 1) * D, :] = placed[:, h * D : (h + 1) * D].T.astype(BF)
-    pos = p_ref[...]
-    pos = digits_row(pos // 128, pos % 128)
-    qt[x, QW:, :] = lax.dot_general(pos, pick, (((1,), (1,)), ((), ())), preferred_element_type=F32).astype(BF)
 
     pl.semaphore_wait(barrier, (NG - 1) + (NZ - 1) + 1 + 3)
 
@@ -131,10 +119,10 @@
 
     def next_row(e, i):
         lane = side if e == 0 else 1 - side
-        return remote(kv.at[lane, 2 * i], kv.at[lane, 2 * i + 1], ns.at[e * 3 + i], nr.at[e * 3 + i], beside)
-
-    rings = [[{s: ring(e, r, s) for s in range(1 + r, 5)} for r in range(2)] for e in range(2)]
-    sides = [[next_row(e, i) for i in range(3)] for e in range(2)]
+        return remote(kv.at[lane, 2 * i], kv.at[lane, 2 * i + 1], ns.at[e * 8 + i], nr.at[e * 8 + i], beside)
+
+    rings = [[{s: ring(e, r, s) for s in ((1, 2, 3, 4), (3,))[r]} for r in range(2)] for e in range(2)]
+    sides = [{i: next_row(e, i) for i in (0, 1, 2, 3, 4, 7)} for e in range(2)]
 
     def launch_first(e):
         if e == 1:
@@ -143,22 +131,22 @@
             copy.start()
         sides[e][0].start()
 
-    def launch_second(e):
-        for i, copy in enumerate(rings[e][0][1]):
+    def launch_later(e, step):
+        for i, copy in enumerate(rings[e][0][step - 1]):
             copy.wait_recv()
-            rings[e][0][2][i].start()
-            sides[e][1 + i].start()
-
-    def launch_second_other(e):
+            rings[e][0][step][i].start()
+            if 2 * step - 3 + i in sides[e]:
+                sides[e][2 * step - 3 + i].start()
+
+    def launch_other(e, step):
         for i in range(2):
-            sides[e][1 + i].wait_recv()
-            rings[e][1][2][i].start()
-
-    def launch_later(e, r, step):
-        for i, copy in enumerate(rings[e][r][step - 1]):
+            sides[e][2 * step - 3 + i].wait_recv()
+            rings[e][1][step][i].start()
+
+    def launch_last(e):
+        for copy in rings[e][0][4]:
             copy.wait_recv()
-        for copy in rings[e][r][step]:
-            copy.start()
+        sides[e][7].start()
 
     def query_copy(k):
         return remote(qt.at[x], qt.at[x], qs.at[k], qr.at[k], at(((x + NX - k) % NX) * NY + y, z))
@@ -168,17 +156,48 @@
         return jnp.minimum(to, NX - 1 - to) <= x
 
     launch_first(0)
-    for k in (1, 3, 2):
-
-        @pl.when(wanted(k))
-        def _():
-            query_copy(k).start()
-
-    launch_first(1)
-
+
+    for load in loads[3:]:
+        load.wait()
+    route = r_ref[...]
+    route = (route // 2 % NZ) * 16 + (route // 16) * 2 + route % 2
+    pick = lax.broadcasted_iota(jnp.int32, (D, D), 0) == jnp.broadcast_to(route, (D, D))
+    pick = jnp.where(pick, 1.0, 0.0).astype(BF)
+    qz_out[:, 0:QW] = jnp.dot(pick, q_ref[...], preferred_element_type=F32).astype(BF)
+    pos = p_ref[...]
+    rows = lax.broadcasted_iota(jnp.int32, (D, D), 0)
+    pos = jnp.where(rows == 0, jnp.broadcast_to(pos // 128, (D, D)), jnp.broadcast_to(pos % 128, (D, D)))
+    pos = jnp.where(rows < 2, pos, 0).astype(F32).T.astype(BF)
+    qz_out[:, QW:] = jnp.dot(pick, pos, preferred_element_type=F32).astype(BF)
+
+    def to_ring(k):
+        to = (z + k) % NZ
+        return remote(qz_out.at[pl.ds(pl.multiple_of(to * 16, 16), 16)], qz.at[z], zs.at[k], zr.at[k], at(g, to))
+
+    turned_queries = [to_ring(k) for k in range(1, NZ)]
+    for copy in turned_queries:
+        copy.start()
+    w_copy.start()
+    qz[z] = qz_out[pl.ds(pl.multiple_of(z * 16, 16), 16), :]
     acc[...] = jnp.zeros_like(acc)
     sm[...] = jnp.zeros_like(sm)
     mx[...] = jnp.full_like(mx, START)
+    launch_first(1)
+
+    for copy in turned_queries:
+        copy.wait_recv()
+    m = lax.broadcasted_iota(jnp.int32, (D, D), 0)
+    n = lax.broadcasted_iota(jnp.int32, (D, D), 1)
+    order = jnp.where(n == (m // 2 % NZ) * 16 + (m // 16) * 2 + m % 2, 1.0, 0.0).astype(BF)
+    placed = jnp.dot(order, qz[...].reshape(D, OW), preferred_element_type=F32)
+    for h in range(HEADS):
+        qt[x, h * D : (h + 1) * D, :] = placed[:, h * D : (h + 1) * D].T.astype(BF)
+    qt[x, QW:, :] = placed[:, QW:].T[0:16, :].astype(BF)
+    for k in (1, 3, 2):
+
+        @pl.when(wanted(k))
+        def _():
+            query_copy(k).start()
 
     def slot_start(e, slot):
         i, r = slot // 2, slot % 2
@@ -188,17 +207,17 @@
         group = low_x if e == 0 else high_x
         return ((group * NY + row) * NZ + ring_at) * (2 * KH) + side * KH
 
-    def turn_ends(first, last):
+    def turn_ends(slots):
         for e in range(2):
-            for slot in range(first, last):
+            for slot in slots:
                 row = kv[e, slot, KH:CUT, :].astype(F32)
                 ends[e, slot] = jnp.broadcast_to(row[0:1, :] * 128.0 + row[1:2, :], (KH, KH)).T
 
-    def flash(b, e, first, last):
+    def flash(b, e, slots):
         row = qt[b, QW : QW + 16, :].astype(F32)
         where = row[0:1, :] * 128.0 + row[1:2, :]
         bias, keys, turned = [], [], []
-        for slot in range(first, last):
+        for slot in slots:
             token = (lax.broadcasted_iota(jnp.int32, (KH, D), 0) + slot_start(e, slot)).astype(F32)
             bias.append(jnp.where((token <= where) & (where < ends[e, slot]), 0.0, MASKED))
             keys.append(kv[e, slot, 0:KH, :])
@@ -226,67 +245,74 @@
             def _():
                 remote(qt.at[b], qt.at[b], qs.at[k], qr.at[k], at(b * NY + y, z)).wait_recv()
 
-            flash(b, 0, 0, 6)
+            flash(b, 0, range(6))
 
         @pl.when(b >= high_x)
         def _():
-            flash(b, 1, 0, 6)
+            flash(b, 1, range(6))
 
         return 0
 
-    def middle_pass(n, _):
-        b = NX - 1 - n
-
+    def middle_pass(slots):
+        def one(n, _):
+            b = NX - 1 - n
+
+            @pl.when(b >= low_x)
+            def _():
+                flash(b, 0, slots)
+
+            @pl.when(b >= high_x)
+            def _():
+                flash(b, 1, slots)
+
+            return 0
+
+        return one
+
+    launch_later(0, 2)
+    launch_later(1, 2)
+    for e in range(2):
+        for i in range(3):
+            sides[e][i].wait_recv()
+    turn_ends(range(6))
+    lax.fori_loop(0, 2, first_pass, 0)
+    launch_later(0, 3)
+    launch_later(1, 3)
+    lax.fori_loop(2, 4, first_pass, 0)
+    launch_later(0, 4)
+    launch_later(1, 4)
+    launch_other(0, 3)
+    launch_other(1, 3)
+    turn_ends(range(6, 10))
+    lax.fori_loop(0, 2, middle_pass(range(6, 10)), 0)
+    launch_last(0)
+    launch_last(1)
+    lax.fori_loop(2, NX, middle_pass(range(6, 10)), 0)
+    turn_ends((10, 12, 14))
+    lax.fori_loop(0, NX, middle_pass((10, 12, 14)), 0)
+    for e in range(2):
+        for copy in rings[e][1][3]:
+            copy.wait_recv()
+        sides[e][7].wait_recv()
+    turn_ends((11, 13, 15))
+
+    def out_rows(group):
+        return pl.ds(pl.multiple_of(group * 16, 16), 16)
+
+    def out_copy(b, k):
+        to = ((x + k // 2) % NX) * NY + (y + k % 2) % NY
+        return remote(
+            osend.at[b, out_rows(to)], orecv.at[x, b * NY + y], os_.at[b * NG + k], or_.at[x * NG + b * NY + y], at(to, z)
+        )
+
+    def finish(b):
         @pl.when(b >= low_x)
         def _():
-            flash(b, 0, 6, 10)
+            flash(b, 0, (11, 13, 15))
 
         @pl.when(b >= high_x)
         def _():
-            flash(b, 1, 6, 10)
-
-        return 0
-
-    launch_second(0)
-    launch_second(1)
-    for e in range(2):
-        sides[e][0].wait_recv()
-    launch_second_other(0)
-    launch_second_other(1)
-    turn_ends(0, 6)
-    lax.fori_loop(0, 2, first_pass, 0)
-    for e in range(2):
-        for r in range(2):
-            launch_later(e, r, 3)
-    turn_ends(6, 10)
-    lax.fori_loop(2, 4, first_pass, 0)
-    for e in range(2):
-        for r in range(2):
-            launch_later(e, r, 4)
-    lax.fori_loop(0, NX, middle_pass, 0)
-    for e in range(2):
-        for r in range(2):
-            for copy in rings[e][r][4]:
-                copy.wait_recv()
-    turn_ends(10, 16)
-
-    def out_copy(b, k):
-        to = (g + k) % NG
-        rows = pl.ds(pl.multiple_of(to * 16, 16), 16)
-        return remote(
-            osend.at[b, rows], orecv.at[x, b * NY + y], os_.at[b * NG + k], or_.at[x * NG + b * NY + y], at(to, z)
-        )
-
-    def last_pass(n, _):
-        b = NX - 1 - n
-
-        @pl.when(b >= low_x)
-        def _():
-            flash(b, 0, 10, 16)
-
-        @pl.when(b >= high_x)
-        def _():
-            flash(b, 1, 10, 16)
+            flash(b, 1, (11, 13, 15))
 
         @pl.when(b >= low_x)
         def _():
@@ -304,104 +330,81 @@
             three = lse - one - two
             table = jnp.concatenate([one, two, three, jnp.zeros((D - 24, D), F32)], 0)
             osend[b, :, QW:] = table.T.astype(BF)
-            for k in range(1, NG):
+            for k in (4, 5, 2, 3, 6, 7, 1):
                 out_copy(b, k).start()
             orecv[x, b * NY + y] = osend[b, pl.ds(pl.multiple_of(g * 16, 16), 16), :]
-
-        return 0
-
-    lax.fori_loop(0, NX, last_pass, 0)
 
     lanes = lax.broadcasted_iota(jnp.int32, (D, QW), 0)
     heads = lax.broadcasted_iota(jnp.int32, (D, QW), 1) // D
     spread = jnp.where((lanes == heads) | (lanes == heads + 8), 1.0, 0.0).astype(BF)
-    used = lax.broadcasted_iota(jnp.int32, (16, D), 1) < 8
-    for b in reversed(range(NG)):
-        sources = [s for s in range(NX) if min(s, NX - 1 - s) <= b // NY]
+
+    def arrive(first, last):
+        for n in range(first, last):
+            for s in range(NX):
+                if min(s, NX - 1 - s) <= n // NY:
+
+                    @pl.when((x != s) | (y != n % NY))
+                    def _():
+                        remote(
+                            orecv.at[s, n], orecv.at[s, n], os_.at[n], or_.at[s * NG + n], at(s * NY + n % NY, z)
+                        ).wait_recv()
+
+    def merge(first, last, sources):
+        size = (last - first) * 16
         lses = []
         for s in sources:
-
-            @pl.when((x != s) | (y != b % NY))
-            def _():
-                remote(
-                    orecv.at[s, b], orecv.at[s, b], os_.at[b], or_.at[s * NG + b], at(s * NY + b % NY, z)
-                ).wait_recv()
-
-            digits = orecv[s, b, :, QW:].astype(F32)
+            digits = orecv[s, first:last, :, QW:].reshape(size, D).astype(F32)
             lses.append(digits + pltpu.roll(digits, D - 8, 1) + pltpu.roll(digits, D - 16, 1))
         best = functools.reduce(jnp.maximum, lses)
         weights = [jnp.exp2(lse - best) for lse in lses]
         total = functools.reduce(jnp.add, weights)
+        used = lax.broadcasted_iota(jnp.int32, (size, D), 1) < 8
         rows = []
         for w in weights:
             w = w / total
             high = w.astype(BF).astype(F32)
             rows.append(jnp.where(used, high, pltpu.roll(w - high, 8, 1)).astype(BF))
         wide = jnp.dot(jnp.concatenate(rows, 0), spread, preferred_element_type=F32)
-        mixed = jnp.zeros((16, QW), F32)
-        for n, s in enumerate(sources):
-            mixed = mixed + orecv[s, b, :, 0:QW].astype(F32) * wide[n * 16 : (n + 1) * 16, :]
-        att[b * 16 : (b + 1) * 16, :] = mixed.astype(BF)
-
+        mixed = jnp.zeros((size, QW), F32)
+        for i, s in enumerate(sources):
+            mixed = mixed + orecv[s, first:last, :, 0:QW].reshape(size, QW).astype(F32) * wide[i * size : (i + 1) * size, :]
+        att[first * 16 : last * 16, :] = mixed.astype(BF)
+
+    def core_copy(b):
+        rows = pl.ds(pl.multiple_of((b * 2 + 1 - tc) * 16, 16), 16)
+        return remote(part.at[rows], crecv.at[b], cs.at[b], cr.at[b], (c, th * 2 + 1 - tc))
+
+    def project(first, last):
+        rows = slice(first * 32, last * 32)
+        for n in range(DOUT // 512):
+            cols = slice(n * 512, (n + 1) * 512)
+            part[rows, cols] = jnp.dot(att[rows, :], w_v[:, cols], preferred_element_type=F32).astype(BF)
+        for b in reversed(range(first, last)):
+            core_copy(b).start()
+
+    def y_copy(b):
+        return remote(ysend.at[b], yall.at[th], ys.at[b], yr.at[th], (c, b * 2 + tc))
+
+    def share(b):
+        core_copy(b).wait_recv()
+        rows = pl.ds(pl.multiple_of((b * 2 + tc) * 16, 16), 16)
+        both = (part[rows, :].astype(F32) + crecv[b].astype(F32)).astype(BF)
+
+        @pl.when(th != b)
+        def _():
+            ysend[b] = both
+            y_copy(b).start()
+
+        @pl.when(th == b)
+        def _():
+            yall[th] = both
+
+    for b in reversed(range(NX)):
+        finish(b)
     w_copy.wait()
-    for n in range(DOUT // 512):
-        cols = slice(n * 512, (n + 1) * 512)
-        part[:, cols] = jnp.dot(att[...], w_v[:, cols], preferred_element_type=F32).astype(BF)
-
-    def rows_of(high, core):
-        return pl.ds(pl.multiple_of((high * 2 + core) * 16, 16), 16)
-
-    core = [
-        remote(part.at[rows_of(j, 1 - tc)], crecv.at[j], cs.at[j], cr.at[j], (c, th * 2 + 1 - tc)) for j in range(4)
-    ]
-    for copy in core:
-        copy.start()
-    along = []
-    for j in range(4):
-        core[j].wait_recv()
-        both = part[rows_of(j, tc), :].astype(F32) + crecv[j].astype(F32)
-
-        ysend[j] = both.astype(BF)
-
-        def across(j=j):
-            return remote(ysend.at[j], yrecv.at[th], ys.at[j], yr.at[th], (c, j * 2 + tc))
-
-        along.append(across)
-
-        @pl.when(th != j)
-        def _():
-            across().start()
-
-        @pl.when(th == j)
-        def _():
-            yrecv[th] = both.astype(BF)
-
-    for j in range(4):
-
-        @pl.when(th != j)
-        def _():
-            remote(yrecv.at[j], yrecv.at[j], ys.at[j], yr.at[j], (c, j * 2 + tc)).wait_recv()
-
-    total = yrecv[0].astype(F32) + yrecv[1].astype(F32) + yrecv[2].astype(F32) + yrecv[3].astype(F32)
-    fin[...] = total
-    for j in range(NZ):
-        zsend[j] = fin[2 * j : 2 * j + 2, :]
-    last = []
-    for k in range(1, NZ):
-        to = (z + k) % NZ
-        copy = remote(zsend.at[to], zrecv.at[z], zs.at[k], zr.at[k], at(g, to))
-        copy.start()
-        last.append(copy)
-    zrecv[z] = zsend[z]
-    for copy in last:
-        copy.wait_recv()
-    for j in range(NZ):
-        fin[2 * j : 2 * j + 2, :] = zrecv[j]
-    out_ref[...] = fin[...].astype(BF)
-
     swap.wait_send()
     for e in range(2):
-        for copy in sides[e]:
+        for copy in sides[e].values():
             copy.wait_send()
         for r in range(2):
             for pair in rings[e][r].values():
@@ -413,6 +416,19 @@
         def _():
             query_copy(k).wait_send()
 
+    for copy in turned_queries:
+        copy.wait_send()
+    arrive(4, 8)
+    merge(4, 8, (0, 1, 2, 3))
+    project(2, 4)
+    share(3)
+    share(2)
+    arrive(0, 4)
+    merge(2, 4, (0, 1, 2, 3))
+    merge(0, 2, (0, 3))
+    project(0, 2)
+    share(1)
+    share(0)
     for b in range(NX):
 
         @pl.when(b >= low_x)
@@ -420,16 +436,20 @@
             for k in range(1, NG):
                 out_copy(b, k).wait_send()
 
-    for copy in core:
-        copy.wait_send()
     for j in range(4):
 
         @pl.when(th != j)
         def _():
-            along[j]().wait_send()
-
-    for copy in last:
-        copy.wait_send()
+            remote(yall.at[j], yall.at[j], ys.at[j], yr.at[j], (c, j * 2 + tc)).wait_recv()
+
+    out_ref[...] = (yall[0].astype(F32) + yall[1].astype(F32) + yall[2].astype(F32) + yall[3].astype(F32)).astype(BF)
+
+    for b in range(NX):
+        core_copy(b).wait_send()
+
+        @pl.when(th != b)
+        def _():
+            y_copy(b).wait_send()
 
 
 def per_device(queries, keys, values, subtree_ends, query_positions, balance_route, out_weight):
@@ -446,6 +466,8 @@
             pltpu.VMEM((2, D), jnp.int32),
             pltpu.VMEM((1, D), jnp.int32),
             pltpu.VMEM((1, D), jnp.int32),
+            pltpu.VMEM((D, OW), BF),
+            pltpu.VMEM((NZ, 16, OW), BF),
             pltpu.VMEM((NX, QR, D), BF),
             pltpu.VMEM((2, 2 * NZ, CR, D), BF),
             pltpu.VMEM((2, 2 * NZ, KH, KH), F32),
@@ -461,14 +483,11 @@
             pltpu.VMEM((4, 16, DOUT), BF),
             pltpu.VMEM((4, 16, DOUT), BF),
             pltpu.VMEM((4, 16, DOUT), BF),
-            pltpu.VMEM((NZ, 2, DOUT), F32),
-            pltpu.VMEM((NZ, 2, DOUT), F32),
-            pltpu.VMEM((16, DOUT), F32),
             dma((6,)), dma,
             dma((NX,)), dma((NX,)),
             dma, dma,
             dma((32,)), dma((32,)),
-            dma((6,)), dma((6,)),
+            dma((16,)), dma((16,)),
             dma((NX * NG,)), dma((NX * NG,)),
             dma((4,)), dma((4,)),
             dma((4,)), dma((4,)),

time: 75.6 us -> 72.4 us (0.958)
  Pallas kernels: 73 us -> 70.3 us
    pallas_call x1, Pallas kernels: 73 us -> 70.3 us  [per_device(): pl.pallas_call(kernel, out_shape=jax.ShapeDtypeStruct((16, DOUT), BF), in...]
where the time goes in v3:
time: 72.4 us; the launch traced here: 71.9 us
  Pallas kernels  70.3 us (97%)
  local copies, waits for them, and re-layouts  1.53 us (2%)
    pallas_call x1, Pallas kernels, per_device(): pl.pallas_call(kernel, out_shape=jax.ShapeDtypeStruct((16, DOUT), BF), in...  70.3 us
    unnamed x1, local copies, waits for them, and re-layouts  1.53 us

profile of v3, /device:TPU:1, one launch (start us, length us, event | category | flops | bytes accessed | tf_op | source)
XLA Modules:
  0.0 71.9 jit_solution(12991129071969504120)
XLA Ops:
  0.0 70.3 %tree_attention.1 = bf16[16,2560]{1,0:T(8,128)(2,1)} custom-call(bf16[128,640]{1,0:T(8,128)(2,1)} %q_in.1, bf16[256,128]{1,0:T(8,128)(2,1)} %k_in.1, bf16[256,128]{1,0:T(8,128)(2,1)} %v_in.1, s32[2,128]{1,0:T(2,128)} %bitcast.2, s32[1,128]{1,0:T(1,128)} %bitcast.3, s32[1,128]{1,0:T(1,128)} %r_in.1, bf16[640,2560]{1,0:T(8,128)(2,1)} %w_in.1), custom_call_target="tpu_custom_call" | custom-call | tf_op jit(solution)/shard_map/tree_attention/pallas_call | solution.py:457
  70.3 1.5 %copy.9 = bf16[16,2560]{1,0:T(8,128)(2,1)} copy(bf16[16,2560]{1,0:T(8,128)(2,1)} %tree_attention.1) | data formatting | bytes 163840

commit v4 on v3

--- a/solution.py
+++ b/solution.py
@@ -245,11 +245,11 @@
             def _():
                 remote(qt.at[b], qt.at[b], qs.at[k], qr.at[k], at(b * NY + y, z)).wait_recv()
 
-            flash(b, 0, range(6))
+            flash(b, 0, (0, 2, 4))
 
         @pl.when(b >= high_x)
         def _():
-            flash(b, 1, range(6))
+            flash(b, 1, (0, 2, 4))
 
         return 0
 
@@ -271,25 +271,28 @@
 
     launch_later(0, 2)
     launch_later(1, 2)
+    turn_ends((0, 2, 4))
+    lax.fori_loop(0, 2, first_pass, 0)
+    launch_later(0, 3)
+    launch_later(1, 3)
+    lax.fori_loop(2, NX, first_pass, 0)
     for e in range(2):
         for i in range(3):
             sides[e][i].wait_recv()
-    turn_ends(range(6))
-    lax.fori_loop(0, 2, first_pass, 0)
-    launch_later(0, 3)
-    launch_later(1, 3)
-    lax.fori_loop(2, 4, first_pass, 0)
+    turn_ends((1, 3, 5))
+    lax.fori_loop(0, 2, middle_pass((1, 3, 5)), 0)
     launch_later(0, 4)
     launch_later(1, 4)
+    lax.fori_loop(2, NX, middle_pass((1, 3, 5)), 0)
     launch_other(0, 3)
     launch_other(1, 3)
-    turn_ends(range(6, 10))
-    lax.fori_loop(0, 2, middle_pass(range(6, 10)), 0)
+    turn_ends((6, 8, 10, 12))
+    lax.fori_loop(0, 2, middle_pass((6, 8, 10, 12)), 0)
     launch_last(0)
     launch_last(1)
-    lax.fori_loop(2, NX, middle_pass(range(6, 10)), 0)
-    turn_ends((10, 12, 14))
-    lax.fori_loop(0, NX, middle_pass((10, 12, 14)), 0)
+    lax.fori_loop(2, NX, middle_pass((6, 8, 10, 12)), 0)
+    turn_ends((7, 9, 14))
+    lax.fori_loop(0, NX, middle_pass((7, 9, 14)), 0)
     for e in range(2):
         for copy in rings[e][1][3]:
             copy.wait_recv()
@@ -399,8 +402,11 @@
         def _():
             yall[th] = both
 
-    for b in reversed(range(NX)):
-        finish(b)
+    def last_pass(n, _):
+        finish(NX - 1 - n)
+        return 0
+
+    lax.fori_loop(0, NX, last_pass, 0)
     w_copy.wait()
     swap.wait_send()
     for e in range(2):

time: 72.4 us -> 69.9 us (0.965)
  Pallas kernels: 70.3 us -> 68.2 us
    pallas_call x1, Pallas kernels: 70.3 us -> 68.2 us  [per_device(): pl.pallas_call(kernel, out_shape=jax.ShapeDtypeStruct((16, DOUT), BF), in...]
where the time goes in v4:
time: 69.9 us; the launch traced here: 69.7 us
  Pallas kernels  68.2 us (98%)
  local copies, waits for them, and re-layouts  1.53 us (2%)
    pallas_call x1, Pallas kernels, per_device(): pl.pallas_call(kernel, out_shape=jax.ShapeDtypeStruct((16, DOUT), BF), in...  68.2 us
    unnamed x1, local copies, waits for them, and re-layouts  1.53 us

profile of v4, /device:TPU:1, one launch (start us, length us, event | category | flops | bytes accessed | tf_op | source)
XLA Modules:
  0.0 69.7 jit_solution(8693784159401607400)
XLA Ops:
  0.0 68.2 %tree_attention.1 = bf16[16,2560]{1,0:T(8,128)(2,1)} custom-call(bf16[128,640]{1,0:T(8,128)(2,1)} %q_in.1, bf16[256,128]{1,0:T(8,128)(2,1)} %k_in.1, bf16[256,128]{1,0:T(8,128)(2,1)} %v_in.1, s32[2,128]{1,0:T(2,128)} %bitcast.2, s32[1,128]{1,0:T(1,128)} %bitcast.3, s32[1,128]{1,0:T(1,128)} %r_in.1, bf16[640,2560]{1,0:T(8,128)(2,1)} %w_in.1), custom_call_target="tpu_custom_call" | custom-call | tf_op jit(solution)/shard_map/tree_attention/pallas_call | solution.py:463
  68.2 1.5 %copy.9 = bf16[16,2560]{1,0:T(8,128)(2,1)} copy(bf16[16,2560]{1,0:T(8,128)(2,1)} %tree_attention.1) | data formatting | bytes 163840
